TPU v7x, 256 devices: a whole 4x4x8 slice. The times are simulated.
256 devices in a mesh: seq: 64 (over z_lo, x, y, core), dp: 4 (over z_hi).
Axes of the slice: x: 4, y: 4, z: 8 (z_hi: 4, z_lo: 2; z = z_hi * 2 + z_lo), core: 2. Of those that a mesh axis runs over, the one named last changes fastest.
Arguments:
- tokens: bfloat16 [4, 262144, 256], P('dp', 'seq'), may hold values from -6 to 6
- cotangent: bfloat16 [4, 262144, 256], P('dp', 'seq'), may hold values from -6 to 6
- first_factor: bfloat16 [512, 512, 512], P('seq', 'dp'), may hold values from -0.25 to 0.25
- second_factor: bfloat16 [512, 512, 512], P('seq', 'dp'), may hold values from -0.25 to 0.25
- hidden_weight: bfloat16 [256, 768], replicated, may hold values from -0.375 to 0.375
- output_weight: bfloat16 [768, 256], replicated, may hold values from -0.21875 to 0.21875
Outputs:
- output: bfloat16 [4, 262144, 256], P('dp', 'seq')
- first_grad: bfloat16 [512, 512, 512], P('seq', 'dp')
- second_grad: bfloat16 [512, 512, 512], P('seq', 'dp')
- hidden_grad: float32 [256, 768], replicated
- output_grad: float32 [768, 256], replicated
All inputs are finite; a program needn't handle non-finite values.
Results may differ from a plain program's by a relative error of at most 0.017.
Values may be sent and summed in bfloat16 or wider, within the bound.
A program may use at most 128 MiB of HBM per device.

v0:
```python
import math

import jax
import jax.numpy as jnp
from jax import lax
from jax.sharding import PartitionSpec as P


def gelu_tanh(value):
    return jax.nn.gelu(value, approximate=True)


def token_work(mixed, inputs, grads, hidden_weight, output_weight):
    gate = jax.nn.silu(inputs.astype(jnp.float32))
    gated = (mixed.astype(jnp.float32) * gate).astype(jnp.bfloat16)
    pre = jnp.dot(gated, hidden_weight, preferred_element_type=jnp.float32)
    active_f, gelu_back = jax.vjp(gelu_tanh, pre)
    activated = active_f.astype(jnp.bfloat16)
    output = (
        gated.astype(jnp.float32)
        + jnp.dot(activated, output_weight, preferred_element_type=jnp.float32)
    ).astype(jnp.bfloat16)
    back = jnp.dot(grads, output_weight.T, preferred_element_type=jnp.float32)
    d_hidden = gelu_back(back)[0].astype(jnp.bfloat16)
    out_part = jnp.dot(activated.T, grads, preferred_element_type=jnp.float32)
    hid_part = jnp.dot(gated.T, d_hidden, preferred_element_type=jnp.float32)
    d_gated = grads.astype(jnp.float32) + jnp.dot(
        d_hidden, hidden_weight.T, preferred_element_type=jnp.float32
    )
    d_mixed = (d_gated * gate).astype(jnp.bfloat16)
    return (output, d_mixed, hid_part, out_part)


def local(tokens, cotangent, first_factor, second_factor, hidden_weight, output_weight):
    local_rows = first_factor.shape[0]
    order = first_factor.shape[2]
    width = tokens.shape[2]
    row_inputs = tokens[0].reshape(local_rows, order, width)
    row_grads = cotangent[0].reshape(local_rows, order, width)
    first_whole = lax.all_gather(first_factor, "dp", axis=1, tiled=True)
    second_whole = lax.all_gather(second_factor, "dp", axis=1, tiled=True)
    first_mixed = jnp.einsum(
        "akb,abc->akc", first_whole, row_inputs, preferred_element_type=jnp.float32
    ).astype(jnp.bfloat16)
    first_cols = lax.all_to_all(first_mixed, "seq", split_axis=1, concat_axis=0, tiled=True)
    mixed_cols = jnp.einsum(
        "kla,akc->lkc", second_whole, first_cols, preferred_element_type=jnp.float32
    ).astype(jnp.bfloat16)
    mixed_rows = lax.all_to_all(mixed_cols, "seq", split_axis=0, concat_axis=1, tiled=True)
    output, d_mixed, hid_part, out_part = token_work(
        mixed_rows.reshape(-1, width),
        row_inputs.reshape(-1, width),
        row_grads.reshape(-1, width),
        hidden_weight,
        output_weight,
    )
    d_cols = lax.all_to_all(
        d_mixed.reshape(local_rows, order, width), "seq", split_axis=1, concat_axis=0, tiled=True
    )
    d_first_cols = jnp.einsum(
        "kla,lkc->akc", second_whole, d_cols, preferred_element_type=jnp.float32
    ).astype(jnp.bfloat16)
    part_second = jnp.einsum("lkc,akc->kla", d_cols, first_cols, preferred_element_type=jnp.float32)
    d_first = lax.all_to_all(d_first_cols, "seq", split_axis=0, concat_axis=1, tiled=True)
    part_first = jnp.einsum("akc,abc->akb", d_first, row_inputs, preferred_element_type=jnp.float32)
    documents = lax.axis_size("dp")
    block_scale = 1.0 / math.sqrt(documents * width)
    weight_scale = 1.0 / math.sqrt(documents * lax.axis_size("seq") * tokens.shape[1])
    first_grad = (
        lax.psum_scatter(
            part_first.astype(jnp.bfloat16), "dp", scatter_dimension=1, tiled=True
        ).astype(jnp.float32)
        * block_scale
    ).astype(jnp.bfloat16)
    second_grad = (
        lax.psum_scatter(
            part_second.astype(jnp.bfloat16), "dp", scatter_dimension=1, tiled=True
        ).astype(jnp.float32)
        * block_scale
    ).astype(jnp.bfloat16)
    hidden_sum, output_sum = lax.psum((hid_part, out_part), ("seq", "dp"))
    return (
        output.reshape(1, -1, width),
        first_grad,
        second_grad,
        hidden_sum * weight_scale,
        output_sum * weight_scale,
    )


def solution(mesh):
    in_specs = (
        P("dp", "seq", None),
        P("dp", "seq", None),
        P("seq", "dp", None),
        P("seq", "dp", None),
        P(),
        P(),
    )
    out_specs = (P("dp", "seq", None), P("seq", "dp", None), P("seq", "dp", None), P(), P())
    return jax.shard_map(local, mesh=mesh, in_specs=in_specs, out_specs=out_specs, check_vma=False)
```

profile of v0, /device:TPU:89, one launch (start us, length us, event | category | flops | bytes accessed | tf_op | source)
XLA Modules:
  0.0 746.1 jit_solution(9767082334986133848)
XLA Ops:
  7.2 0.0 copy-start
  7.2 0.0 all-gather.3.cloned.1.call-start
  7.2 0.7 all-gather.3.cloned.1.call-update
  7.9 0.0 all-gather.5.cloned.1.call-start
  8.0 0.7 all-gather.5.cloned.1.call-update
  8.7 89.6 %all-gather.3.cloned.1.call-done = bf16[8,512,512]{2,1,0:T(8,128)(2,1)} async-done(((bf16[8,128,512]{2,1,0:T(8,128)(2,1)}), bf16[8,512,512]{2,1,0:T(8,128)(2,1)}) %all-gather.3.cloned.1.call-update) | async-done | bytes 4194320 | tf_op jit(solution)/shard_map/all_gather | solution.py:40
  98.3 4.1 convolution_convert_fusion.2
  102.4 1.2 copy.48
  103.6 85.5 %all_to_all.63 = bf16[8,512,256]{2,0,1:T(8,128)(2,1)S(1)} all-to-all(bf16[8,512,256]{2,0,1:T(8,128)(2,1)S(1)} %copy.48), channel_id=1, replica_groups=mesh['seq'=64,'dp'=4] {'seq'}, dimensions={1} | all-to-all | bytes 4194304 | tf_op jit(solution)/shard_map/all_to_all | solution.py:45
  189.1 0.7 copy.50
  189.8 14.1 %all-gather.5.cloned.1.call-done = bf16[8,512,512]{2,1,0:T(8,128)(2,1)} async-done(((bf16[8,128,512]{2,1,0:T(8,128)(2,1)}), bf16[8,512,512]{2,1,0:T(8,128)(2,1)}) %all-gather.5.cloned.1.call-update) | async-done | bytes 4194320 | tf_op jit(solution)/shard_map/all_gather | solution.py:41
  203.9 5.1 convert_bitcast_fusion.2
  209.0 4.5 copy.52
  213.5 35.2 %all_to_all.64 = bf16[512,8,256]{2,1,0:T(8,128)(2,1)S(1)} all-to-all(bf16[512,8,256]{2,1,0:T(8,128)(2,1)} %copy.52), channel_id=1, replica_groups=mesh['seq'=64,'dp'=4] {'seq'}, dimensions={0} | all-to-all | bytes 4194304 | tf_op jit(solution)/shard_map/all_to_all | solution.py:49
  248.8 0.5 convert_bitcast_fusion
  249.3 0.0 copy-start.6
  249.3 0.4 copy.53
  249.7 1.2 copy-done.6
  250.9 1.6 fusion.14
  252.5 0.0 copy-done
  252.5 0.0 copy-start.4
  252.6 0.0 copy-start.8
  252.6 0.0 copy-start.10
  252.6 5.9 multiply_convert_fusion
  258.5 0.0 copy-done.4
  258.5 0.0 copy-done.8
  258.5 0.0 copy-done.10
  258.5 9.6 %fusion.6 = bf16[4096,768]{1,0:T(8,128)(2,1)S(1)} fusion(f32[4096,768]{1,0:T(8,128)S(1)} %get-tuple-element.8, bf16[768,256]{1,0:T(8,128)(2,1)S(1)} %copy-done.10, bf16[1,4096,256]{2,1,0:T(8,128)(2,1)S(1)} %copy-done.8), kind=kOutput, calls=%fused_computation.8 | convolution fusion | flops 1673527296 | bytes 21364736 | tf_op jit(solution)/shard_map/dot_general | solution.py:23
  268.0 0.0 copy-start.1
  268.1 2.3 fusion.9
  270.4 0.3 copy-done.1
  270.6 2.5 copy.54
  273.1 7.9 %all-to-all-start.2 = ((bf16[8,512,256]{2,0,1:T(8,128)(2,1)}), bf16[8,512,256]{2,0,1:T(8,128)(2,1)}, u32[]{:S(2)}, u32[]{:S(2)}) async-start(bf16[8,512,256]{2,0,1:T(8,128)(2,1)} %copy.54), calls=%async_computation.2 | async-start | bytes 4194304 | tf_op jit(solution)/shard_map/all_to_all | solution.py:57
  281.0 0.3 all-reduce.3.cloned.1.call-start
  281.3 0.0 copy-start.9
  281.3 6.3 fusion.24
  287.6 0.0 copy-done.9
  287.6 5.5 fusion.16
  293.1 0.0 all-reduce.3.cloned.1.call-update
  293.1 0.0 reduce-scatter.5.cloned.1.call-start
  293.1 15.1 %all-to-all-done.2 = bf16[8,512,256]{2,0,1:T(8,128)(2,1)} async-done(((bf16[8,512,256]{2,0,1:T(8,128)(2,1)}), bf16[8,512,256]{2,0,1:T(8,128)(2,1)}, u32[]{:S(2)}, u32[]{:S(2)}) %all-to-all-start.2) | async-done | bytes 2097184 | tf_op jit(solution)/shard_map/all_to_all | solution.py:57
  308.2 2.3 copy.56
  310.5 0.0 copy-start.2
  310.5 1.3 copy-done.2
  311.8 3.6 convolution_convert_fusion
  315.5 0.0 reduce-scatter.5.cloned.1.call-update
  315.5 0.0 reduce-scatter.3.cloned.1.call-start
  315.5 1.5 copy-done.3
  317.1 4.9 convert_bitcast_fusion.1
  321.9 3.3 copy.58
  325.3 0.0 copy-start.7
  325.3 36.4 %all_to_all.65 = bf16[512,8,256]{2,1,0:T(8,128)(2,1)S(1)} all-to-all(bf16[512,8,256]{2,1,0:T(8,128)(2,1)S(1)} %copy.58), channel_id=1, replica_groups=mesh['seq'=64,'dp'=4] {'seq'}, dimensions={0} | all-to-all | bytes 4194304 | tf_op jit(solution)/shard_map/all_to_all | solution.py:64
  361.7 0.0 copy-done.7
  361.7 3.4 convolution_convert_fusion.1
  365.1 0.0 reduce-scatter.3.cloned.1.call-update
  365.1 1.6 copy-done.5
  366.6 5.9 fusion.10
  372.6 194.8 %all-reduce.3.cloned.1.call-done = (f32[256,768]{1,0:T(8,128)}, f32[768,256]{1,0:T(8,128)}) async-done(((f32[256,768]{1,0:T(8,128)}, f32[768,256]{1,0:T(8,128)}), (f32[256,768]{1,0:T(8,128)}, f32[768,256]{1,0:T(8,128)})) %all-reduce.3.cloned.1.call-update) | async-done | bytes 1572880 | tf_op jit(solution)/shard_map/psum | solution.py:81
  567.4 2.1 broadcast_multiply_fusion.1
  569.4 2.1 broadcast_multiply_fusion
  571.5 80.7 %reduce-scatter.5.cloned.1.call-done = bf16[8,128,512]{2,1,0:T(8,128)(2,1)} async-done(((bf16[8,512,512]{2,1,0:T(8,128)(2,1)}), bf16[8,128,512]{2,1,0:T(8,128)(2,1)}) %reduce-scatter.5.cloned.1.call-update) | async-done | bytes 1048592 | tf_op jit(solution)/shard_map/reduce_scatter | solution.py:76
  652.2 2.4 multiply_convert_fusion.1
  654.6 82.6 %reduce-scatter.3.cloned.1.call-done = bf16[8,128,512]{2,1,0:T(8,128)(2,1)} async-done(((bf16[8,512,512]{2,1,0:T(8,128)(2,1)}), bf16[8,128,512]{2,1,0:T(8,128)(2,1)}) %reduce-scatter.3.cloned.1.call-update) | async-done | bytes 1048592 | tf_op jit(solution)/shard_map/reduce_scatter | solution.py:70
  737.2 2.4 multiply_convert_fusion.2
  (2 shorter events, 0.0 us)
Async XLA Ops:
  7.2 245.4 %copy-start = (bf16[256,768]{1,0:T(8,128)(2,1)S(1)}, bf16[256,768]{1,0:T(8,128)(2,1)}, u32[]{:S(2)}) copy-start(bf16[256,768]{1,0:T(8,128)(2,1)} %param.10) | copy-start | bytes 1179652
  7.2 91.1 %all-gather.3.cloned.1.call-start = ((), (), s32[]{:S(2)}) async-start(), calls=%async_computation.6 | async-start | bytes 5242880 | tf_op jit(solution)/shard_map/all_gather | solution.py:40
  7.9 196.0 %all-gather.5.cloned.1.call-start = ((), (), s32[]{:S(2)}) async-start(), calls=%async_computation.7 | async-start | bytes 5242880 | tf_op jit(solution)/shard_map/all_gather | solution.py:41
  249.3 1.6 copy-start.6
  252.5 5.9 copy-start.4
  252.6 5.9 copy-start.8
  252.6 5.9 copy-start.10
  268.0 2.6 copy-start.1
  273.1 35.1 %all-to-all-start.2 = ((bf16[8,512,256]{2,0,1:T(8,128)(2,1)}), bf16[8,512,256]{2,0,1:T(8,128)(2,1)}, u32[]{:S(2)}, u32[]{:S(2)}) async-start(bf16[8,512,256]{2,0,1:T(8,128)(2,1)} %copy.54), calls=%async_computation.2 | async-start | bytes 4194304 | tf_op jit(solution)/shard_map/all_to_all | solution.py:57
  281.0 286.4 %all-reduce.3.cloned.1.call-start = ((), (), s32[]{:S(2)}) async-start(), calls=%async_computation.10 | async-start | bytes 3145728 | tf_op jit(solution)/shard_map/psum | solution.py:81
  281.3 6.3 copy-start.9
  293.1 359.1 %reduce-scatter.5.cloned.1.call-start = ((), (), s32[]{:S(2)}) async-start(), calls=%async_computation.9 | async-start | bytes 5242880 | tf_op jit(solution)/shard_map/reduce_scatter | solution.py:76
  310.5 1.3 copy-start.2
  315.5 1.6 copy-start.3
  315.5 421.7 %reduce-scatter.3.cloned.1.call-start = ((), (), s32[]{:S(2)}) async-start(), calls=%async_computation.8 | async-start | bytes 5242880 | tf_op jit(solution)/shard_map/reduce_scatter | solution.py:70
  325.3 36.4 %copy-start.7 = (bf16[1,4096,256]{2,1,0:T(8,128)(2,1)S(1)}, bf16[1,4096,256]{2,1,0:T(8,128)(2,1)}, u32[]{:S(2)}) copy-start(bf16[1,4096,256]{2,1,0:T(8,128)(2,1)} %param.6) | copy-start | bytes 6291460
  365.1 1.6 copy-start.5
Sparse Core Ops, SparseCore 0:
  9.8 88.4 all-gather.2
  100.1 103.7 all-gather.4
  293.2 274.1 all-reduce.2
  570.0 82.1 reduce-scatter.4
  654.6 82.5 reduce-scatter.2
where the time goes:
time: 751 us; the launch traced here: 746 us
  waiting for transfers between devices  478 us (64%)
  blocking collectives  157 us (21%)
  matrix products  56.5 us (8%)
  local copies, waits for them, and re-layouts  20.8 us (3%)
  between operations  14 us (2%)
  other arithmetic  11.1 us (1%)
  starting transfers between devices  8.29 us (1%)
    psum x1, waiting for transfers between devices, local(): hidden_sum, output_sum = lax.psum((hid_part, out_part), ('seq', 'dp'))  195 us
    all_gather x1, waiting for transfers between devices, local(): first_whole = lax.all_gather(first_factor, 'dp', axis=1, tiled=True)  89.6 us
    all_to_all x1, blocking collectives, local(): lax.all_to_all(first_mixed, 'seq', split_axis=1, concat_axis=0, tiled=True)  85.5 us
    reduce_scatter x1, waiting for transfers between devices, local(): lax.psum_scatter(part_first.astype(jnp.bfloat16), 'dp', scatter_dimension...  82.6 us
    reduce_scatter x1, waiting for transfers between devices, local(): lax.psum_scatter(part_second.astype(jnp.bfloat16), 'dp', scatter_dimensio...  80.7 us
    all_to_all x1, blocking collectives, local(): lax.all_to_all(d_first_cols, 'seq', split_axis=0, concat_axis=1, tiled=True)  36.4 us
    all_to_all x1, blocking collectives, local(): lax.all_to_all(mixed_cols, 'seq', split_axis=0, concat_axis=1, tiled=True)  35.2 us
    all_to_all x1, waiting for transfers between devices, local(): lax.all_to_all(d_mixed.reshape(local_rows, order, width), 'seq', split_ax...  15.1 us
  transfers between devices with their start and end apart: 6, of which 6 were waited for; matrix products, arithmetic and copies ran while one was open for 6% of the time, Pallas kernels for 0%

commit v1 on v0

v1 whole, which is shorter than its diff:
```python
import functools
import math

import jax
import jax.numpy as jnp
from jax import lax
from jax.experimental import pallas as pl
from jax.experimental.pallas import tpu as pltpu
from jax.sharding import PartitionSpec as P

MESH = pl.DeviceIdType.MESH
BF = jnp.bfloat16
F32 = jnp.float32
DMA = pltpu.SemaphoreType.DMA
ANY = pl.BlockSpec(memory_space=pl.ANY)
VM = pl.BlockSpec(memory_space=pltpu.VMEM)
BLOCK_SCALE = 1.0 / math.sqrt(1024.0)
WEIGHT_SCALE = 1.0 / math.sqrt(1048576.0)


def dev(s, p):
    return {"seq": s, "dp": p}


def offset(s, i):
    z, x, y, c = s // 32, (s // 8) % 4, (s // 2) % 4, s % 2
    j = i // 2
    z = (z + i) % 2
    x = (x + j) % 4
    y = (y + j // 4 + j) % 4
    c = (c + j // 16) % 2
    return z * 32 + x * 8 + y * 2 + c


def place():
    s, p = lax.axis_index("seq"), lax.axis_index("dp")
    z, b = s // 32, (s // 16) % 2
    mate = p + 1 - 2 * (p % 2)
    twin = s + 16 * (1 - 2 * b)
    same = (z + b) % 2 == (p + p // 2) % 2
    return s, p, z, b, mate, 3 - p, twin, same


def remote(src, dst, ssem, rsem, s, p):
    return pltpu.make_async_remote_copy(src, dst, ssem, rsem, device_id=dev(s, p), device_id_type=MESH)


def drain(ref, sem):
    pltpu.make_async_copy(ref, ref, sem).wait()


def loop(n, body, start=0):
    def step(i, carry):
        body(i)
        return carry

    lax.fori_loop(start, n, step, 0)


def dot(a, b, dims=((1,), (0,))):
    return lax.dot_general(a, b, (dims, ((), ())), preferred_element_type=F32)


def front_kernel(
    x_ref, f_ref, s_ref, perm_ref, fm_ref, sp_ref, xp_ref,
    xown, xmate, f2, fmx, out, load, xs, xr, fs, fr, sas, sar, sbs, sbr, ms, mr, tail,
):
    s, p, z, b, mate, cross, twin, same = place()
    side = p // 2
    odd = p % 2
    pltpu.make_async_copy(x_ref, xown, load.at[0]).start()
    pltpu.make_async_copy(f_ref, f2.at[:, side], load.at[1]).start()
    bar = pltpu.get_barrier_semaphore()

    def greet(t, q):
        pl.semaphore_signal(bar, 1, device_id=dev(t, q), device_id_type=MESH)

    greet(s, mate)
    greet(s, cross)
    greet(twin, mate)
    loop(64, lambda i: greet(offset(s, i), p), 1)
    pl.semaphore_wait(bar, 66)

    remote(f_ref, f2.at[:, side], fs, fr, s, cross).start()
    dest = jnp.where(same, p, mate)
    remote(s_ref.at[1 - b], sp_ref.at[:, p], sas.at[0], sar, twin, dest).start()

    @pl.when(same)
    def _():
        pltpu.make_async_copy(s_ref.at[b], sp_ref.at[:, p], sar).start()

    @pl.when(jnp.logical_not(same))
    def _():
        remote(s_ref.at[b], sp_ref.at[:, p], sas.at[1], sar, s, mate).start()

    loop(8, lambda a: remote(x_ref.at[a], xmate.at[a], xs, xr.at[a], s, mate).start())

    def mix(e, x):
        def one(a):
            fmx[a] = dot(f2[a].reshape(256, 512), x[a]).astype(BF)

        return one

    def spread(e):
        def group(g):
            rows = fmx[:, pl.ds(pl.multiple_of(g * 32, 32), 32), :].reshape(256, 256)
            turned = dot(perm_ref[...], rows).astype(BF).reshape(8, 32, 256)
            out[e, pl.ds(g * 8, 8)] = turned

        loop(8, group)
        pltpu.make_async_copy(out.at[e, s], fm_ref.at[e, s], mr).start()

        def send(i):
            t = offset(s, i)
            remote(out.at[e, t], fm_ref.at[e, s], ms, mr, t, p).start()

        loop(64, send, 1)

    pltpu.make_async_copy(x_ref, xown, load.at[0]).wait()
    pltpu.make_async_copy(f_ref, f2.at[:, side], load.at[1]).wait()
    drain(f2.at[:, 1 - side], fr)
    loop(8, mix(odd, xown))
    spread(odd)
    drain(sp_ref.at[:, pl.ds(0, 2)], sar)
    half = sp_ref.at[:, pl.ds(2 * side, 2)]
    remote(half, half, sbs, sbr, s, cross).start()

    def arrive(a):
        drain(xmate.at[a], xr.at[a])
        pltpu.make_async_copy(xmate.at[a], xp_ref.at[a], tail).start()
        mix(1 - odd, xmate)(a)

    loop(8, arrive)
    spread(1 - odd)
    drain(x_ref, xs)
    drain(f_ref, fs)
    drain(s_ref.at[0], sas.at[0])

    @pl.when(jnp.logical_not(same))
    def _():
        drain(s_ref.at[0], sas.at[1])

    drain(xmate, tail)
    drain(sp_ref.at[:, pl.ds(0, 2)], sbs)
    drain(sp_ref.at[:, pl.ds(0, 2)], sbr)
    drain(out.at[:, pl.ds(0, 63)], ms)
    drain(out, mr)


def front(x, f, second, perm):
    return pl.pallas_call(
        front_kernel,
        out_shape=(
            jax.ShapeDtypeStruct((2, 64, 32, 256), BF),
            jax.ShapeDtypeStruct((4, 4, 128, 512), BF),
            jax.ShapeDtypeStruct((8, 512, 256), BF),
        ),
        in_specs=[ANY, ANY, ANY, VM],
        out_specs=(ANY, ANY, ANY),
        scratch_shapes=[
            pltpu.VMEM((8, 512, 256), BF),
            pltpu.VMEM((8, 512, 256), BF),
            pltpu.VMEM((8, 2, 128, 512), BF),
            pltpu.VMEM((8, 256, 256), BF),
            pltpu.VMEM((2, 64, 32, 256), BF),
            DMA((2,)), DMA, DMA((8,)), DMA, DMA, DMA((2,)), DMA, DMA, DMA, DMA, DMA, DMA,
        ],
        compiler_params=pltpu.CompilerParams(
            collective_id=1, has_side_effects=True, vmem_limit_bytes=40 << 20
        ),
    )(x, f, second, perm)


def token_tile(mixed, x, grads, w1, w2, w1t, w2t):
    xf = x.astype(F32)
    gate = xf / (1.0 + jnp.exp(-xf))
    gated = (mixed.astype(F32) * gate).astype(BF)
    pre = dot(gated, w1)
    root = math.sqrt(2.0 / math.pi)
    square = pre * pre
    tanh = jnp.tanh(pre * (root + (root * 0.044715) * square))
    half = 0.5 * (1.0 + tanh)
    activated = (pre * half).astype(BF)
    slope = half + 0.5 * pre * (1.0 - tanh * tanh) * (root + (3.0 * root * 0.044715) * square)
    output = (gated.astype(F32) + dot(activated, w2)).astype(BF)
    d_hidden = (dot(grads, w2t) * slope).astype(BF)
    out_part = dot(grads, activated, ((0,), (0,)))
    hid_part = dot(gated, d_hidden, ((0,), (0,)))
    d_mixed = ((grads.astype(F32) + dot(d_hidden, w1t)) * gate).astype(BF)
    return output, d_mixed, hid_part, out_part


def back_kernel(
    fm_ref, sp_ref, xo_ref, xp_ref, xt_ref, ct_ref, w1, w2, w1t, w2t, perm_ref,
    out_ref, fg_ref, sg_ref, wg_ref,
    fm, sp, xe, xt, ct, fmk, dmk, mb, mr, db, dr, ob, dfb, dfr, dfa, gb, gr, go, fgb, fgr, fgo,
    acc, rsb, zb, agb,
    load, mbs, mrs, dbs, drs, dfbs, dfrs, gbs, grs, gos, gor, fgs, fgrs, rss, rsr, zbs, zbr, ags, agr, tail,
):
    s, p, z, b, mate, cross, twin, same = place()
    side, odd = p // 2, p % 2
    kind = (p + p // 2) % 2
    base = 2 * side
    copies = [
        (fm_ref, fm), (sp_ref, sp), (xt_ref, xt), (ct_ref, ct),
        (xo_ref, xe.at[:, :, pl.ds(pl.multiple_of(256 * odd, 256), 256)]),
        (xp_ref, xe.at[:, :, pl.ds(pl.multiple_of(256 * (1 - odd), 256), 256)]),
    ]
    for n, (src, dst) in enumerate(copies):
        pltpu.make_async_copy(src, dst, load.at[n]).start()

    def loaded(n):
        pltpu.make_async_copy(copies[n][0], copies[n][1], load.at[n]).wait()

    bar = pltpu.get_barrier_semaphore()

    def greet(t, q):
        pl.semaphore_signal(bar, 1, device_id=dev(t, q), device_id_type=MESH)

    flip = s + 32 * (1 - 2 * z)
    for q in (2 - base, 3 - base):
        greet(s, q)
        greet(flip, q)
    greet(s, mate)

    def hello(i):
        greet(offset(s, i), p)
        greet(offset(s, i), mate)

    loop(64, hello, 1)

    loaded(0)
    loaded(1)

    def columns(src, dst, n):
        def piece(t):
            for e in range(2):
                rows = src(e, t).astype(F32)
                for i in range(2):
                    dst[n + i, pl.ds(pl.multiple_of(t * 128, 128), 128), 256 * e:256 * e + 256] = (
                        rows[:, 8 * i:8 * i + 8, :].reshape(128, 256).astype(BF)
                    )

        loop(4, piece)

    for j in range(2):
        columns(lambda e, t: fm[e, pl.ds(t * 16, 16), 16 * j:16 * j + 16, :], fmk, 2 * j)
    pl.semaphore_wait(bar, 131)

    for j in range(2):
        def second(t):
            parts = [
                dot(sp[2 * j + i, t], fmk[2 * j + i]).reshape(16, 8, 512) for i in range(2)
            ]
            whole = jnp.concatenate(parts, axis=1).astype(BF)
            for e in range(2):
                mb[j, pl.ds(t * 16, 16), e] = whole[:, :, 256 * e:256 * e + 256]

        loop(4, second)
        pltpu.make_async_copy(mb.at[j, s, odd], mr.at[j, kind, s // 8, s % 8], mrs.at[j]).start()

        def send(i):
            t = offset(s, i)
            remote(mb.at[j, t, 1 - odd], mr.at[j, kind, s // 8, s % 8], mbs.at[j], mrs.at[j], t, mate).start()

            @pl.when(i > 0)
            def _():
                remote(mb.at[j, t, odd], mr.at[j, kind, s // 8, s % 8], mbs.at[j], mrs.at[j], t, p).start()

        loop(64, send)

    acc[...] = jnp.zeros_like(acc)
    loaded(2)
    loaded(3)
    for j in range(2):
        drain(mr.at[j], mrs.at[j])

        def tile(n):
            lo = (s + n) % 8
            mixed = mr[j, :, :, lo].reshape(256, 256)
            x = xt[j, :, :, lo].reshape(256, 256)
            grads = ct[j, :, :, lo].reshape(256, 256)
            output, d_mixed, hid_part, out_part = token_tile(
                mixed, x, grads, w1[...], w2[...], w1t[...], w2t[...]
            )
            ob[j, :, :, lo] = output.reshape(2, 8, 16, 256)
            db[j, :, :, lo] = d_mixed.reshape(2, 8, 16, 256)
            acc[0:16] += hid_part.reshape(16, 16, 768)
            acc[16:32] += out_part.reshape(16, 16, 768)

            def send(m):
                hi = (s // 8 + m) % 8
                t = hi * 8 + lo
                remote(db.at[j, 1 - kind, hi, lo], dr.at[j, odd, s], dbs.at[j], drs.at[j], t, mate).start()
                here = t == s

                @pl.when(here)
                def _():
                    pltpu.make_async_copy(db.at[j, kind, hi, lo], dr.at[j, odd, s], drs.at[j]).start()

                @pl.when(jnp.logical_not(here))
                def _():
                    remote(db.at[j, kind, hi, lo], dr.at[j, odd, s], dbs.at[j], drs.at[j], t, p).start()

            loop(8, send)

        loop(8, tile)
        pltpu.make_async_copy(ob.at[j], out_ref.at[j], tail.at[0]).start()

    w = s % 32
    pltpu.make_async_copy(acc.at[w], rsb.at[w], rsr).start()

    def scatter(i):
        t = (w + i) % 32
        remote(acc.at[t], rsb.at[w], rss, rsr, z * 32 + t, p).start()

    loop(32, scatter, 1)

    for j in range(2):
        drain(dr.at[j], drs.at[j])
        columns(lambda e, t: dr[j, e, pl.ds(t * 16, 16)], dmk, 0)

        def grads_of(t):
            for i in range(2):
                rows = dmk[i, pl.ds(pl.multiple_of(t * 128, 128), 128), :]
                gb[2 * j + i, t] = dot(rows, fmk[2 * j + i], ((1,), (1,))).astype(BF)

        loop(4, grads_of)
        remote(
            gb.at[pl.ds(2 * j, 2), pl.ds(2 - base, 2)], gr.at[pl.ds(2 * j, 2)],
            gbs.at[j], grs.at[j], s, cross,
        ).start()

        def first_back(t):
            parts = []
            for i in range(2):
                weights = sp[2 * j + i, :, :, pl.ds(pl.multiple_of(t * 128, 128), 128)].reshape(512, 128)
                parts.append(dot(weights, dmk[i], ((0,), (0,))).reshape(16, 8, 512))
            whole = jnp.concatenate(parts, axis=1).astype(BF)
            for e in range(2):
                dfb[j, pl.ds(t * 16, 16), e] = whole[:, :, 256 * e:256 * e + 256]

        loop(4, first_back)
        pltpu.make_async_copy(dfb.at[j, s], dfr.at[j, s], dfrs.at[j]).start()

        def send(i):
            t = offset(s, i)
            remote(dfb.at[j, t], dfr.at[j, s], dfbs.at[j], dfrs.at[j], t, p).start()

        loop(64, send, 1)

    drain(rsb, rsr)
    plane = 2 * p + z
    zb[plane] = jnp.sum(rsb[...], axis=0)
    for q in range(4):
        for u in range(2):
            @pl.when(plane != 2 * q + u)
            def _():
                remote(zb.at[plane], zb.at[plane], zbs, zbr, u * 32 + w, q).start()

    loaded(4)
    loaded(5)
    for j in range(2):
        drain(dfr.at[j], dfrs.at[j])

        def turn(g):
            for e in range(2):
                rows = dfr[j, pl.ds(g * 16, 16), e].reshape(256, 256)
                turned = dot(perm_ref[...], rows).astype(BF).reshape(8, 32, 256)
                dfa[:, pl.ds(pl.multiple_of(g * 32, 32), 32), 256 * e:256 * e + 256] = turned

        loop(4, turn)

        def first_grad(a):
            fgb[j, a] = dot(dfa[a], xe[a], ((1,), (1,))).astype(BF).reshape(2, 64, 512)

        loop(8, first_grad)
        remote(fgb.at[j, :, 1 - side], fgr.at[j], fgs.at[j], fgrs.at[j], s, cross).start()

    drain(zb.at[pl.ds(0, 7)], zbr)
    agb[w] = jnp.sum(zb[...], axis=0) * WEIGHT_SCALE

    def gather(i):
        remote(agb.at[w], agb.at[w], ags, agr, z * 32 + (w + i) % 32, p).start()

    loop(32, gather, 1)

    for j in range(2):
        drain(gr.at[pl.ds(2 * j, 2)], grs.at[j])

    def second_sum(k):
        mine = gb[k, pl.ds(base, 2)].astype(F32)
        go[k] = ((mine + gr[k].astype(F32)) * BLOCK_SCALE).astype(BF)

    loop(4, second_sum)
    home = jnp.where(same, s, twin)
    remote(go.at[:, 1 - odd], sg_ref.at[b], gos.at[0], gor, home, mate).start()

    @pl.when(same)
    def _():
        pltpu.make_async_copy(go.at[:, odd], sg_ref.at[b], gor).start()

    @pl.when(jnp.logical_not(same))
    def _():
        remote(go.at[:, odd], sg_ref.at[b], gos.at[1], gor, twin, p).start()

    for j in range(2):
        drain(fgr.at[j], fgrs.at[j])

        def first_sum(a):
            mine = fgb[j, a, side].astype(F32)
            fgo[j, a] = ((mine + fgr[j, a].astype(F32)) * BLOCK_SCALE).astype(BF)

        loop(8, first_sum)
    pltpu.make_async_copy(fgo, fg_ref, tail.at[1]).start()
    drain(agb.at[pl.ds(0, 31)], agr)
    pltpu.make_async_copy(agb, wg_ref, tail.at[2]).start()

    for j in range(2):
        drain(mr.at[j, 0], mbs.at[j])
        drain(mr.at[j, 0, pl.ds(0, 7)], mbs.at[j])
        drain(mr.at[j, 0, 0, pl.ds(0, 7)], mbs.at[j])
        drain(mr.at[j, 0], dbs.at[j])
        drain(mr.at[j, 0, pl.ds(0, 7)], dbs.at[j])
        drain(mr.at[j, 0, 0, pl.ds(0, 7)], dbs.at[j])
        drain(dfb.at[j, pl.ds(0, 63)], dfbs.at[j])
        drain(gr.at[pl.ds(2 * j, 2)], gbs.at[j])
        drain(fgr.at[j], fgs.at[j])
    drain(rsb.at[pl.ds(0, 31)], rss)
    drain(zb.at[pl.ds(0, 7)], zbs)
    drain(agb.at[pl.ds(0, 31)], ags)
    drain(go.at[:, 0], gos.at[0])

    @pl.when(jnp.logical_not(same))
    def _():
        drain(go.at[:, 0], gos.at[1])

    drain(sg_ref, gor)
    drain(ob, tail.at[0])
    drain(fgo, tail.at[1])
    drain(agb, tail.at[2])


def back(fm, sp, xo, xp, xt, ct, w1, w2, w1t, w2t, perm):
    half = (2, 2, 8, 8, 16, 256)
    return pl.pallas_call(
        back_kernel,
        out_shape=(
            jax.ShapeDtypeStruct(half, BF),
            jax.ShapeDtypeStruct((2, 8, 64, 512), BF),
            jax.ShapeDtypeStruct((2, 4, 128, 512), BF),
            jax.ShapeDtypeStruct((32, 16, 768), F32),
        ),
        in_specs=[ANY] * 6 + [VM] * 5,
        out_specs=(ANY,) * 4,
        scratch_shapes=[
            pltpu.VMEM((2, 64, 32, 256), BF),
            pltpu.VMEM((4, 4, 128, 512), BF),
            pltpu.VMEM((8, 512, 512), BF),
            pltpu.VMEM(half, BF),
            pltpu.VMEM(half, BF),
            pltpu.VMEM((4, 512, 512), BF),
            pltpu.VMEM((2, 512, 512), BF),
            pltpu.VMEM((2, 64, 2, 16, 256), BF),
            pltpu.VMEM(half, BF),
            pltpu.VMEM(half, BF),
            pltpu.VMEM((2, 2, 64, 16, 256), BF),
            pltpu.VMEM(half, BF),
            pltpu.VMEM((2, 64, 2, 16, 256), BF),
            pltpu.VMEM((2, 64, 2, 16, 256), BF),
            pltpu.VMEM((8, 128, 512), BF),
            pltpu.VMEM((4, 4, 128, 512), BF),
            pltpu.VMEM((4, 2, 128, 512), BF),
            pltpu.VMEM((4, 2, 128, 512), BF),
            pltpu.VMEM((2, 8, 2, 64, 512), BF),
            pltpu.VMEM((2, 8, 64, 512), BF),
            pltpu.VMEM((2, 8, 64, 512), BF),
            pltpu.VMEM((32, 16, 768), F32),
            pltpu.VMEM((32, 16, 768), F32),
            pltpu.VMEM((8, 16, 768), F32),
            pltpu.VMEM((32, 16, 768), F32),
            DMA((6,)), DMA((2,)), DMA((2,)), DMA((2,)), DMA((2,)), DMA((2,)), DMA((2,)),
            DMA((2,)), DMA((2,)), DMA((2,)), DMA, DMA((2,)), DMA((2,)),
            DMA, DMA, DMA, DMA, DMA, DMA, DMA((3,)),
        ],
        compiler_params=pltpu.CompilerParams(
            collective_id=2, has_side_effects=True, vmem_limit_bytes=58 << 20
        ),
    )(fm, sp, xo, xp, xt, ct, w1, w2, w1t, w2t, perm)


def by_column(rows):
    parts = rows.reshape(8, 4, 16, 2, 2, 2, 256)
    parts = jnp.concatenate([parts[:, 0:1], parts[:, 3:4], parts[:, 1:3]], axis=1)
    return parts.transpose(4, 1, 3, 2, 5, 0, 6).reshape(2, 2, 8, 8, 16, 256)


def by_row(columns):
    parts = columns.reshape(2, 4, 2, 16, 2, 8, 256).transpose(5, 1, 3, 2, 0, 4, 6)
    parts = jnp.concatenate([parts[:, 0:1], parts[:, 2:4], parts[:, 1:2]], axis=1)
    return parts.reshape(1, 4096, 256)


def local(tokens, cotangent, first_factor, second_factor, hidden_weight, output_weight):
    x = tokens[0].reshape(8, 512, 256)
    f = first_factor.reshape(8, 16, 2, 4, 512).transpose(0, 2, 1, 3, 4).reshape(8, 128, 512)
    second = second_factor.reshape(2, 4, 128, 512)
    row = lax.broadcasted_iota(jnp.int32, (256, 256), 0)
    col = lax.broadcasted_iota(jnp.int32, (256, 256), 1)
    to_column = (col == (row % 8) * 32 + row // 8).astype(BF)
    to_row = (col == (row % 32) * 8 + row // 32).astype(BF)
    fm, sp, xp = front(x, f, second, to_column)
    out, fg, sg, wg = back(
        fm, sp, x, xp, by_column(tokens), by_column(cotangent),
        hidden_weight, output_weight, hidden_weight.T, output_weight.T, to_row,
    )
    first_grad = fg.reshape(2, 8, 2, 16, 2, 512).transpose(1, 3, 2, 0, 4, 5).reshape(8, 128, 512)
    wg = wg.reshape(2, 256, 768)
    return by_row(out), first_grad, sg.reshape(8, 128, 512), wg[0], wg[1].T


def solution(mesh):
    in_specs = (
        P("dp", "seq", None),
        P("dp", "seq", None),
        P("seq", "dp", None),
        P("seq", "dp", None),
        P(),
        P(),
    )
    out_specs = (P("dp", "seq", None), P("seq", "dp", None), P("seq", "dp", None), P(), P())
    return jax.shard_map(local, mesh=mesh, in_specs=in_specs, out_specs=out_specs, check_vma=False)
```

time: 751 us -> 394 us (0.52)
  waiting for transfers between devices: 478 us -> 0 us
  Pallas kernels: 0 us -> 347 us
  blocking collectives: 157 us -> 0 us
  matrix products: 56.5 us -> 0 us
  local copies, waits for them, and re-layouts: 20.8 us -> 36.4 us
  between operations: 14 us -> 0.9 us
  starting transfers between devices: 8.29 us -> 0 us
    pallas_call x0 -> x2, Pallas kernels: none -> 347 us  [the longest x1 201 us: back(): pl.pallas_call(back_kernel, out_shape=(jax.ShapeDtypeStruct(half, BF), ja...]
    psum x1 -> x0, waiting for transfers between devices: 195 us -> none  [local(): hidden_sum, output_sum = lax.psum((hid_part, out_part), ('seq', 'dp'))]
    reduce_scatter x2 -> x0, waiting for transfers between devices: 163 us -> none  [the longest x1 82.6 us: local(): lax.psum_scatter(part_first.astype(jnp.bfloat16), 'dp', scatter_dimension...]
    all_to_all x3 -> x0, blocking collectives: 157 us -> none  [the longest x1 85.5 us: local(): lax.all_to_all(first_mixed, 'seq', split_axis=1, concat_axis=0, tiled=True)]
    all_gather x2 -> x0, waiting for transfers between devices: 104 us -> none  [the longest x1 89.6 us: local(): first_whole = lax.all_gather(first_factor, 'dp', axis=1, tiled=True)]
    dot_general x11 -> x0, matrix products: 56.5 us -> none  [the longest x1 9.57 us: token_work(): back = jnp.dot(grads, output_weight.T, preferred_element_type=jnp.float32)]
    all_to_all x1 -> x0, waiting for transfers between devices: 15.1 us -> none  [local(): lax.all_to_all(d_mixed.reshape(local_rows, order, width), 'seq', split_ax...]
    unnamed x22 -> x29, local copies, waits for them, and re-layouts: 5.97 us -> 16 us
  transfers between devices with their start and end apart: 6 -> 0, of which waited for: 6 -> 0; matrix products, arithmetic and copies ran while one was open for 6% -> 0% of each run, Pallas kernels for 0% -> 0%
where the time goes in v1:
time: 394 us; the launch traced here: 389 us
  Pallas kernels  347 us (88%)
  local copies, waits for them, and re-layouts  36.4 us (9%)
  other arithmetic  4.6 us (1%)
    pallas_call x1, Pallas kernels, back(): pl.pallas_call(back_kernel, out_shape=(jax.ShapeDtypeStruct(half, BF), ja...  201 us
    pallas_call x1, Pallas kernels, front(): pl.pallas_call(front_kernel, out_shape=(jax.ShapeDtypeStruct((2, 64, 32,...  146 us
    unnamed x29, local copies, waits for them, and re-layouts  16 us

profile of v1, /device:TPU:89, one launch (start us, length us, event | category | flops | bytes accessed | tf_op | source)
XLA Modules:
  0.0 388.7 jit_solution(2692741043874697619)
XLA Ops:
  0.6 0.0 copy-start.7
  0.7 0.3 fusion.perm_ref
  1.0 0.9 fusion.1.perm_ref
  1.9 1.9 copy.18
  3.8 1.9 copy.19
  5.8 0.0 copy-done.7
  5.8 0.3 reshape.51
  6.0 0.5 copy.30
  6.5 0.3 reshape.52.f_ref
  6.8 2.8 reshape.56
  9.6 0.8 slice.51
  10.4 0.7 fusion.10
  11.1 0.6 copy.26
  11.7 1.1 copy.28
  12.8 0.6 copy.27
  13.4 0.0 copy-start
  13.4 1.6 pad_maximum_fusion.1
  15.0 0.8 copy-done
  15.7 2.2 reshape.54
  17.9 0.0 copy-start.5
  17.9 1.6 copy-done.5
  19.5 0.0 slice-start
  19.5 0.9 fusion.11
  20.4 0.6 copy.23
  20.9 0.0 slice-done
  21.0 1.1 copy.25
  22.1 0.6 copy.24
  22.7 0.0 copy-start.4
  22.7 1.5 pad_maximum_fusion
  24.2 0.0 copy-done.4
  24.2 146.0 %shard_map.101 = (bf16[2,64,32,256]{3,2,1,0:T(8,128)(2,1)S(1)}, bf16[4,4,128,512]{3,2,1,0:T(8,128)(2,1)S(1)}, bf16[8,512,256]{2,1,0:T(8,128)(2,1)S(1)}) custom-call(bf16[8,512,256]{2,1,0:T(8,128)(2,1)S(1)} %bitcast.24, bf16[8,128,512]{2,1,0:T(8,128)(2,1)S(1)} %reshape.52.f_ref, bf16[2,4,128,512]{3,2,1,0:T(8,128)(2,1)S(1)} %bitcast.25, ...), custom_call_target="tpu_custom_call" | custom-call | tf_op jit(solution)/shard_map/pallas_call | solution.py:151
  170.2 0.0 copy-start.1
  170.2 1.3 copy-done.1
  171.5 0.0 copy-start.2
  171.5 1.3 copy-done.2
  172.8 0.0 copy-start.3
  172.8 1.3 copy-done.3
  174.1 200.8 %shard_map.102 = (bf16[2,2,8,8,16,256]{5,4,3,2,1,0:T(8,128)(2,1)}, bf16[2,8,64,512]{3,2,1,0:T(8,128)(2,1)}, bf16[2,4,128,512]{3,2,1,0:T(8,128)(2,1)}, f32[32,16,768]{2,1,0:T(8,128)}) custom-call(bf16[2,64,32,256]{3,2,1,0:T(8,128)(2,1)} %copy-done.1, bf16[4,4,128,512]{3,2,1,0:T(8,128)(2,1)} %copy-done.2, bf16[8,512,256]{2,1,0:T(8,128)(2,1)} %bitcast.23, ...), custom_call_target="tpu_custom_call" | custom-call | tf_op jit(solution)/shard_map/pallas_call | solution.py:446
  375.0 0.0 copy-start.6
  375.0 1.4 slice.53
  376.4 0.4 copy-done.6
  376.9 0.1 fusion.9
  377.0 0.2 pad_maximum_fusion.2
  377.2 2.2 copy.20
  379.4 0.0 copy-start.9
  379.4 2.2 reshape.59
  381.6 0.0 copy-done.9
  381.7 0.4 reshape.60
  382.1 0.8 copy.21
  382.9 1.2 reshape.61
  384.1 0.0 copy-start.8
  384.1 2.4 fusion.12
  386.6 1.1 copy.22
  387.7 0.0 copy-done.8
  387.7 1.0 copy.32
  (6 shorter events, 0.0 us)
Async XLA Ops:
  0.6 5.1 %copy-start.7 = (bf16[8,128,512]{2,1,0:T(8,128)(2,1)S(1)}, bf16[8,128,512]{2,1,0:T(8,128)(2,1)}, u32[]{:S(2)}) copy-start(bf16[8,128,512]{2,1,0:T(8,128)(2,1)} %param.8) | copy-start | bytes 3145732
  13.4 2.4 copy-start
  17.9 1.6 copy-start.5
  19.5 1.4 slice-start
  22.7 1.6 copy-start.4
  170.2 1.3 copy-start.1
  171.5 1.3 copy-start.2
  172.8 1.3 copy-start.3
  375.0 1.9 copy-start.6
  379.4 2.2 copy-start.9
  384.1 3.6 copy-start.8

commit v2 on v0

v2 whole, which is shorter than its diff:
```python
import math

import jax
import jax.numpy as jnp
import numpy as np
from jax import lax
from jax.experimental import pallas as pl
from jax.experimental.pallas import tpu as pltpu
from jax.sharding import PartitionSpec as P

MESH = pl.DeviceIdType.MESH
BF = jnp.bfloat16
F32 = jnp.float32
DMA = pltpu.SemaphoreType.DMA
ANY = pl.BlockSpec(memory_space=pl.ANY)
VM = pl.BlockSpec(memory_space=pltpu.VMEM)
BLOCK_SCALE = 1.0 / math.sqrt(1024.0)
WEIGHT_SCALE = 1.0 / math.sqrt(1048576.0)
SINGLES = (
    "lx", "lf", "lc", "f_s", "f_r", "sa_s0", "sa_s1", "sa_r", "sb_s", "sb_r", "x_s0", "x_s1", "x_r0", "x_r1",
    "a1_s", "a1_ra", "a1_rb", "a2_sa", "a2_ra", "a3_sa", "a3_ra", "a4_sa", "a4_ra",
    "go_r", "rs_s", "rs_r", "zl_s", "zl_r", "z_s", "z_r", "ag_s", "ag_r", "t_out", "t_first", "t_hid", "t_wide",
)
FOURS = ("a2_s", "a2_r", "a3_s", "a3_r", "a4_s", "a4_r", "g_s", "g_r", "h_s", "h_r", "go_s0", "go_s1")


def dev(s, p):
    return {"seq": s, "dp": p}


def offset(s, i):
    z, x, y, c = s // 32, (s // 8) % 4, (s // 2) % 4, s % 2
    j = i // 2
    z = (z + i) % 2
    x = (x + j) % 4
    y = (y + j // 4 + j) % 4
    c = (c + j // 16) % 2
    return z * 32 + x * 8 + y * 2 + c


def remote(src, dst, ssem, rsem, s, p):
    return pltpu.make_async_remote_copy(src, dst, ssem, rsem, device_id=dev(s, p), device_id_type=MESH)


def drain(ref, sem):
    pltpu.make_async_copy(ref, ref, sem).wait()


def loop(n, body, start=0):
    def step(i, carry):
        body(i)
        return carry

    lax.fori_loop(start, n, step, 0)


def rows_at(start, n):
    return pl.ds(pl.multiple_of(start, n), n)


def dot(a, b, dims=((1,), (0,))):
    return lax.dot_general(a, b, (dims, ((), ())), preferred_element_type=F32)


def pack(rows):
    tiles = rows.reshape(-1, 8, 256)
    return jnp.concatenate([tiles[:, :, :128], tiles[:, :, 128:]], axis=1).astype(BF)


def unpack(tiles):
    tiles = tiles.reshape(-1, 16, 128).astype(F32)
    return jnp.concatenate([tiles[:, :8], tiles[:, 8:]], axis=2).reshape(-1, 256)


def token_tile(mixed, xf, grads, w1, w2, w1t, w2t):
    gate = xf / (1.0 + jnp.exp(-xf))
    gated = (mixed * gate).astype(BF)
    pre = dot(gated, w1)
    root = math.sqrt(2.0 / math.pi)
    square = pre * pre
    tanh = jnp.tanh(pre * (root + (root * 0.044715) * square))
    half = 0.5 * (1.0 + tanh)
    activated = (pre * half).astype(BF)
    slope = half + 0.5 * pre * (1.0 - tanh * tanh) * (root + (3.0 * root * 0.044715) * square)
    output = gated.astype(F32) + dot(activated, w2)
    low = grads.astype(BF)
    d_hidden = (dot(low, w2t) * slope).astype(BF)
    out_part = dot(low, activated, ((0,), (0,)))
    hid_part = dot(gated, d_hidden, ((0,), (0,)))
    d_mixed = (grads + dot(d_hidden, w1t)) * gate
    return output, d_mixed, hid_part, out_part


def kernel(
    x_ref, c_ref, f_ref, s_ref, w1, w2, to_col, to_row, to_block, to_k,
    out_ref, fg_ref, sg_ref, hid_ref, wide_ref,
    xe, raw, f2, fmx, fs, fm, fmk, sp, st, xt, ct, ob, mb, mr, db, dr, dmk, dfb, dfr, dfa,
    gb, gr, go, fgb, fgr, fgo, acc, rsb, zl, zb, agb, wide, w1t, w2t, single, fours,
):
    one = {name: single.at[n] for n, name in enumerate(SINGLES)}
    four = {name: fours.at[n] for n, name in enumerate(FOURS)}
    s, p = lax.axis_index("seq"), lax.axis_index("dp")
    z, b = s // 32, (s // 16) % 2
    mate, cross = p + 1 - 2 * (p % 2), 3 - p
    twin, flip = s + 16 * (1 - 2 * b), s + 32 * (1 - 2 * z)
    side, odd = p // 2, p % 2
    kind = (p + side) % 2
    same = (z + b) % 2 == kind
    unlike = jnp.logical_not(same)
    base = 2 * side

    load_x = pltpu.make_async_copy(x_ref, xe.at[:, :, 0:256], one["lx"])
    load_f = pltpu.make_async_copy(f_ref, f2.at[:, side], one["lf"])
    load_c = pltpu.make_async_copy(c_ref, raw, one["lc"])
    load_x.start()
    load_f.start()
    load_c.start()

    bar = pltpu.get_barrier_semaphore()

    def greet(t, q):
        pl.semaphore_signal(bar, 1, device_id=dev(t, q), device_id_type=MESH)

    greet(s, mate)
    for q in (2 - base, 3 - base):
        greet(s, q)
        greet(flip, q)

    def hello(i):
        greet(offset(s, i), p)
        greet(offset(s, i), mate)

    loop(64, hello, 1)
    pl.semaphore_wait(bar, 131)

    remote(f_ref, f2.at[:, side], one["f_s"], one["f_r"], s, cross).start()
    dest = jnp.where(same, p, mate)
    remote(s_ref.at[1 - b], sp.at[:, p], one["sa_s0"], one["sa_r"], twin, dest).start()

    @pl.when(same)
    def _():
        pltpu.make_async_copy(s_ref.at[b], sp.at[:, p], one["sa_r"]).start()

    @pl.when(unlike)
    def _():
        remote(s_ref.at[b], sp.at[:, p], one["sa_s1"], one["sa_r"], s, mate).start()

    def x_half(n):
        lanes = slice(128 * n, 128 * n + 128)
        return remote(
            x_ref.at[:, :, lanes], xe.at[:, :, 256 + 128 * n:384 + 128 * n], one[f"x_s{n}"], one[f"x_r{n}"], s, mate
        )

    x_half(0).start()

    w1t[...] = w1[...].T
    w2t[...] = w2[...].T

    def to_columns(src, dst):
        def group(n):
            q, rg = n // 4, n % 4
            rel = (q // 2 + q % 2 + kind) % 2
            rows = src[:, rows_at(n * 32, 32), 0:256].reshape(256, 256)
            tiles = pack(dot(to_col[...], rows)).reshape(2, 4, 4, 16, 128)
            for h in range(2):
                dst[rel, (q // 2) * 4 + h * 2 + rg // 2, pl.ds((rg % 2) * 4, 4)] = tiles[h]

        loop(16, group)

    load_x.wait()
    to_columns(xe, xt)
    load_c.wait()
    to_columns(raw, ct)
    acc[...] = jnp.zeros_like(acc)

    def first_mix(e, lane, width):
        def block(a):
            fmx[a, :, 0:width] = dot(f2[a].reshape(256, 512), xe[a, :, 256 * e + lane:256 * e + lane + width]).astype(BF)

        loop(8, block)

        def group(n):
            q, rg = n // 4, n % 4
            rows = fmx[:, rows_at(n * 32, 32), 0:width].reshape(256, width)
            tiles = dot(to_col[...], rows).astype(BF).reshape(2, 4, 32, width)
            for h in range(2):
                fs[e, pl.ds(q * 32 + h * 16 + rg * 4, 4), :, lane:lane + width] = tiles[h]

        loop(8, group)
        lanes = slice(lane, lane + width)
        rsem = one["a1_rb" if e else "a1_ra"]
        pltpu.make_async_copy(fs.at[e, s, :, lanes], fm.at[e, s, :, lanes], rsem).start()

        def send(i):
            t = offset(s, i)
            remote(fs.at[e, t, :, lanes], fm.at[e, s, :, lanes], one["a1_s"], rsem, t, p).start()

        loop(64, send, 1)

    load_f.wait()
    drain(f2.at[:, 1 - side], one["f_r"])
    first_mix(0, 0, 256)
    drain(sp.at[:, pl.ds(0, 2)], one["sa_r"])
    half = sp.at[:, pl.ds(base, 2)]
    remote(half, half, one["sb_s"], one["sb_r"], s, cross).start()
    x_half(0).wait_send()
    x_half(1).start()
    x_half(0).wait_recv()
    first_mix(1, 0, 128)

    def mixed_columns(e):
        def piece(t):
            rows = fm[e, pl.ds(t * 16, 16)].astype(F32)
            for k in range(4):
                fmk[k, rows_at(t * 128, 128), 256 * e:256 * e + 256] = (
                    rows[:, 8 * k:8 * k + 8, :].reshape(128, 256).astype(BF)
                )

        loop(4, piece)

    def second_mix(e, k):
        def piece(t):
            mb[e, pl.ds(t * 16, 16), k] = pack(dot(sp[k, t], fmk[k, :, 256 * e:256 * e + 256]))

        loop(4, piece)

    drain(sp.at[:, pl.ds(0, 2)], one["sb_r"])
    drain(fs.at[0], one["a1_ra"])
    mixed_columns(0)
    for k in range(4):
        second_mix(0, k)
    pltpu.make_async_copy(mb.at[0, s], mr.at[0, s // 8, s % 8], one["a2_ra"]).start()

    def send_own(i):
        t = offset(s, i)
        remote(mb.at[0, t], mr.at[0, s // 8, s % 8], one["a2_sa"], one["a2_ra"], t, p).start()

    loop(64, send_own, 1)

    def turn_second(k):
        for t in range(4):
            for u in range(4):
                st[k, u, :, 128 * t:128 * t + 128] = sp[k, t, :, 128 * u:128 * u + 128].T

    loop(4, turn_second)

    x_half(1).wait_recv()
    first_mix(1, 128, 128)

    def tokens(rel, pick, shape):
        output, d_mixed, hid_part, out_part = token_tile(
            unpack(pick(mr)[...]), unpack(pick(xt)[...]), unpack(pick(ct)[...]), w1[...], w2[...], w1t[...], w2t[...]
        )
        pick(ob)[...] = pack(output).reshape(shape)
        pick(db)[...] = pack(d_mixed).reshape(shape)
        acc[0:16] += hid_part.reshape(16, 16, 768)
        acc[16:32] += out_part.reshape(16, 16, 768)

    drain(mb.at[0], one["a2_ra"])

    def own_tile(n):
        lo = (s + n) % 8
        tokens(0, lambda ref: ref.at[0, :, lo], (8, 4, 16, 128))

        def send(m):
            hi = (s // 8 + m) % 8
            t = hi * 8 + lo
            here = t == s

            @pl.when(here)
            def _():
                pltpu.make_async_copy(db.at[0, hi, lo], dr.at[0, s], one["a3_ra"]).start()

            @pl.when(jnp.logical_not(here))
            def _():
                remote(db.at[0, hi, lo], dr.at[0, s], one["a3_sa"], one["a3_ra"], t, p).start()

        loop(8, send)

    loop(4, own_tile)

    drain(fs.at[1], one["a1_rb"])
    mixed_columns(1)

    def mate_mix(k):
        second_mix(1, k)

        def send(i):
            t = offset(s, i)
            remote(mb.at[1, t, k], mr.at[1, s // 8, s % 8, k], four["a2_s"].at[k], four["a2_r"].at[k], t, mate).start()

        loop(64, send)

    for k in range(4):
        mate_mix(k)
    loop(8, own_tile, 4)

    def d_columns(e, k):
        def piece(t):
            dmk[k, rows_at(t * 128, 128), 256 * e:256 * e + 256] = unpack(dr[e, pl.ds(t * 16, 16), k]).astype(BF)

        loop(4, piece)

    def first_back(e, k):
        def piece(t):
            dfb[e, pl.ds(t * 16, 16), k] = pack(dot(st[k, t], dmk[k, :, 256 * e:256 * e + 256]))

        loop(4, piece)

    def own_back():
        drain(mb.at[0], one["a3_ra"])
        for k in range(4):
            d_columns(0, k)
            first_back(0, k)
        pltpu.make_async_copy(dfb.at[0, s], dfr.at[0, s], one["a4_ra"]).start()

        def send(i):
            t = offset(s, i)
            remote(dfb.at[0, t], dfr.at[0, s], one["a4_sa"], one["a4_ra"], t, p).start()

        loop(64, send, 1)

    def mate_tokens(k):
        drain(mb.at[1, :, k], four["a2_r"].at[k])

        def tile(n):
            lo = 4 * ((s // 4 + n) % 2)
            tokens(1, lambda ref: ref.at[1, :, pl.ds(lo, 4), k], (8, 4, 16, 128))

            def send(m):
                t = ((s // 8 + m) % 8) * 8 + lo + (s + m // 8) % 4
                remote(
                    db.at[1, t // 8, t % 8, k], dr.at[1, s, k], four["a3_s"].at[k], four["a3_r"].at[k], t, mate
                ).start()

            loop(32, send)

        loop(2, tile)

    def mate_back(k):
        drain(mb.at[1, :, k], four["a3_r"].at[k])
        d_columns(1, k)

        def piece(t):
            gb[k, t] = dot(dmk[k, rows_at(t * 128, 128), :], fmk[k], ((1,), (1,))).astype(BF)

        loop(4, piece)
        remote(gb.at[k, pl.ds(2 - base, 2)], gr.at[k], four["g_s"].at[k], four["g_r"].at[k], s, cross).start()
        first_back(1, k)
        pltpu.make_async_copy(dfb.at[1, s, k], dfr.at[1, s, k], four["a4_r"].at[k]).start()

        def send(i):
            t = offset(s, i)
            remote(dfb.at[1, t, k], dfr.at[1, s, k], four["a4_s"].at[k], four["a4_r"].at[k], t, p).start()

        loop(64, send, 1)

    def first_grad(k):
        drain(dfb.at[1, :, k], four["a4_r"].at[k])
        for e in range(2):
            for g in range(2):
                rows = unpack(dfr[e, 32 * g:32 * g + 32, k]).astype(BF)
                dfa[:, 32 * g:32 * g + 32, 256 * e:256 * e + 256] = (
                    dot(to_block[...], rows).astype(BF).reshape(8, 32, 256)
                )

        def block(a):
            fgb[k, :, a] = dot(dfa[a], xe[a], ((1,), (1,))).astype(BF).reshape(2, 32, 512)

        loop(8, block)
        remote(fgb.at[k, 1 - side], fgr.at[k], four["h_s"].at[k], four["h_r"].at[k], s, cross).start()

    def second_sum(k):
        drain(gr.at[k], four["g_r"].at[k])
        mine = gb[k, pl.ds(base, 2)].astype(F32)
        go[k] = ((mine + gr[k].astype(F32)) * BLOCK_SCALE).astype(BF)
        home = jnp.where(same, s, twin)
        remote(go.at[k, 1 - odd], sg_ref.at[4 * b + k], four["go_s0"].at[k], one["go_r"], home, mate).start()

        @pl.when(same)
        def _():
            pltpu.make_async_copy(go.at[k, odd], sg_ref.at[4 * b + k], one["go_r"]).start()

        @pl.when(unlike)
        def _():
            remote(go.at[k, odd], sg_ref.at[4 * b + k], four["go_s1"].at[k], one["go_r"], twin, p).start()

    w = s % 32

    def reduce_start():
        pltpu.make_async_copy(acc.at[w], rsb.at[w], one["rs_r"]).start()

        def send(i):
            t = (w + i) % 32
            remote(acc.at[t], rsb.at[w], one["rs_s"], one["rs_r"], z * 32 + t, p).start()

        loop(32, send, 1)

    def reduce_pair():
        drain(rsb, one["rs_r"])
        zl[0] = jnp.sum(rsb[...], axis=0)
        remote(zl.at[0], zl.at[1], one["zl_s"], one["zl_r"], flip, p).start()

    def reduce_planes():
        drain(zl.at[1], one["zl_r"])
        zb[p] = zl[0] + zl[1]
        for i in range(1, 4):
            remote(zb.at[p], zb.at[p], one["z_s"], one["z_r"], s, (p + i) % 4).start()

    def reduce_gather():
        drain(zb.at[pl.ds(0, 3)], one["z_r"])
        agb[w] = jnp.sum(zb[...], axis=0) * WEIGHT_SCALE

        def send(i):
            remote(agb.at[w], agb.at[w], one["ag_s"], one["ag_r"], z * 32 + (w + i) % 32, p).start()

        loop(32, send, 1)

    own_back()
    mate_tokens(0)
    mate_tokens(1)
    mate_back(0)
    mate_tokens(2)
    mate_back(1)
    drain(dfb.at[0], one["a4_ra"])
    first_grad(0)
    mate_tokens(3)
    reduce_start()
    mate_back(2)
    first_grad(1)
    second_sum(0)
    mate_back(3)
    reduce_pair()
    first_grad(2)
    second_sum(1)
    reduce_planes()
    first_grad(3)
    second_sum(2)
    reduce_gather()

    def to_rows(n):
        q, rg = n // 4, n % 4
        rel = (q // 2 + q % 2 + kind) % 2
        lo = (rg % 2) * 4
        hi = (q // 2) * 4 + rg // 2
        tiles = jnp.concatenate([ob[rel, hi, pl.ds(lo, 4)], ob[rel, hi + 2, pl.ds(lo, 4)]], axis=0)
        rows = dot(to_row[...], unpack(tiles).astype(BF)).astype(BF)
        raw[:, rows_at(n * 32, 32), :] = rows.reshape(8, 32, 256)

    loop(16, to_rows)
    for n in range(8):
        pltpu.make_async_copy(raw.at[n], out_ref.at[0, pl.ds(512 * n, 512)], one["t_out"]).start()

    second_sum(3)
    drain(agb.at[pl.ds(0, 31)], one["ag_r"])
    pltpu.make_async_copy(agb.at[pl.ds(0, 16)], hid_ref, one["t_hid"]).start()
    for n in range(6):
        wide[128 * n:128 * n + 128, :] = agb[16:32, :, 128 * n:128 * n + 128].reshape(256, 128).T
    pltpu.make_async_copy(wide, wide_ref, one["t_wide"]).start()

    for k in range(4):
        drain(fgr.at[k], four["h_r"].at[k])

    def first_sum(a):
        total = (fgb[:, side, a].astype(F32) + fgr[:, a].astype(F32)) * BLOCK_SCALE
        fgo[a] = dot(to_k[...], total.astype(BF).reshape(128, 512)).astype(BF)

    loop(8, first_sum)
    pltpu.make_async_copy(fgo, fg_ref, one["t_first"]).start()

    drain(f_ref, one["f_s"])
    drain(s_ref.at[0], one["sa_s0"])

    @pl.when(unlike)
    def _():
        drain(s_ref.at[0], one["sa_s1"])
        for k in range(4):
            drain(go.at[k, 0], four["go_s1"].at[k])

    drain(half, one["sb_s"])
    x_half(1).wait_send()
    drain(fs.at[:, pl.ds(0, 63)], one["a1_s"])
    for name in ("a2_sa", "a3_sa", "a4_sa"):
        drain(mb.at[0, pl.ds(0, 63)], one[name])
    for k in range(4):
        drain(mb.at[1, :, k], four["a2_s"].at[k])
        drain(mb.at[1, :, k], four["a3_s"].at[k])
        drain(mb.at[1, pl.ds(0, 63), k], four["a4_s"].at[k])
        drain(gr.at[k], four["g_s"].at[k])
        drain(fgr.at[k], four["h_s"].at[k])
        drain(go.at[k, 0], four["go_s0"].at[k])
    drain(rsb.at[pl.ds(0, 31)], one["rs_s"])
    drain(zl.at[0], one["zl_s"])
    drain(zb.at[pl.ds(0, 3)], one["z_s"])
    drain(agb.at[pl.ds(0, 31)], one["ag_s"])
    drain(sg_ref, one["go_r"])
    drain(raw, one["t_out"])
    drain(fgo, one["t_first"])
    drain(agb.at[pl.ds(0, 16)], one["t_hid"])
    drain(wide, one["t_wide"])


def permutation(*shape_and_order):
    shape, order = shape_and_order
    places = np.arange(math.prod(shape)).reshape(shape).transpose(order).reshape(-1)
    return np.eye(places.size, dtype=np.float32)[places]


def local(tokens, cotangent, first_factor, second_factor, hidden_weight, output_weight):
    to_col = permutation((8, 4, 2, 4), (2, 1, 3, 0))
    to_block = permutation((32, 8), (1, 0))
    to_k = permutation((4, 2, 16), (2, 1, 0))
    tiles = (2, 8, 8, 4, 16, 128)
    pieces = (2, 64, 4, 16, 128)
    scratch = [
        ((8, 512, 512), BF), ((8, 512, 256), BF), ((8, 2, 128, 512), BF), ((8, 256, 256), BF),
        ((2, 64, 32, 256), BF), ((2, 64, 32, 256), BF), ((4, 512, 512), BF),
        ((4, 4, 128, 512), BF), ((4, 4, 128, 512), BF),
        (tiles, BF), (tiles, BF), (tiles, BF), (pieces, BF), (tiles, BF), (tiles, BF), (pieces, BF),
        ((4, 512, 512), BF), (pieces, BF), (pieces, BF), ((8, 64, 512), BF),
        ((4, 4, 128, 512), BF), ((4, 2, 128, 512), BF), ((4, 2, 128, 512), BF),
        ((4, 2, 8, 32, 512), BF), ((4, 8, 32, 512), BF), ((8, 128, 512), BF),
        ((32, 16, 768), F32), ((32, 16, 768), F32), ((2, 16, 768), F32), ((4, 16, 768), F32), ((32, 16, 768), F32),
        ((768, 256), F32), ((768, 256), BF), ((256, 768), BF),
    ]
    out, fg, sg, hid, wide = pl.pallas_call(
        kernel,
        out_shape=(
            jax.ShapeDtypeStruct((1, 4096, 256), BF),
            jax.ShapeDtypeStruct((8, 128, 512), BF),
            jax.ShapeDtypeStruct((8, 128, 512), BF),
            jax.ShapeDtypeStruct((16, 16, 768), F32),
            jax.ShapeDtypeStruct((768, 256), F32),
        ),
        in_specs=[ANY] * 4 + [VM] * 6,
        out_specs=(ANY,) * 5,
        scratch_shapes=[pltpu.VMEM(*shape) for shape in scratch]
        + [DMA((len(SINGLES),)), DMA((len(FOURS), 4))],
        compiler_params=pltpu.CompilerParams(
            collective_id=1, has_side_effects=True, vmem_limit_bytes=62 << 20
        ),
    )(
        tokens.reshape(8, 512, 256), cotangent.reshape(8, 512, 256), first_factor,
        second_factor.reshape(2, 4, 128, 512), hidden_weight, output_weight,
        jnp.asarray(to_col, BF), jnp.asarray(to_col.T, BF), jnp.asarray(to_block, BF), jnp.asarray(to_k, BF),
    )
    return out, fg, sg, hid.reshape(256, 768), wide


def solution(mesh):
    in_specs = (
        P("dp", "seq", None),
        P("dp", "seq", None),
        P("seq", "dp", None),
        P("seq", "dp", None),
        P(),
        P(),
    )
    out_specs = (P("dp", "seq", None), P("seq", "dp", None), P("seq", "dp", None), P(), P())
    return jax.shard_map(local, mesh=mesh, in_specs=in_specs, out_specs=out_specs, check_vma=False)
```

time: 751 us -> 363 us (0.48)
  waiting for transfers between devices: 478 us -> 0 us
  Pallas kernels: 0 us -> 352 us
  blocking collectives: 157 us -> 0 us
  matrix products: 56.5 us -> 0 us
  local copies, waits for them, and re-layouts: 20.8 us -> 6.91 us
  between operations: 14 us -> 0.66 us
  other arithmetic: 11.1 us -> 0 us
  starting transfers between devices: 8.29 us -> 0 us
    pallas_call x0 -> x1, Pallas kernels: none -> 352 us  [local(): pl.pallas_call(kernel, out_shape=(jax.ShapeDtypeStruct((1, 4096, 256), BF...]
    psum x1 -> x0, waiting for transfers between devices: 195 us -> none  [local(): hidden_sum, output_sum = lax.psum((hid_part, out_part), ('seq', 'dp'))]
    reduce_scatter x2 -> x0, waiting for transfers between devices: 163 us -> none  [the longest x1 82.6 us: local(): lax.psum_scatter(part_first.astype(jnp.bfloat16), 'dp', scatter_dimension...]
    all_to_all x3 -> x0, blocking collectives: 157 us -> none  [the longest x1 85.5 us: local(): lax.all_to_all(first_mixed, 'seq', split_axis=1, concat_axis=0, tiled=True)]
    all_gather x2 -> x0, waiting for transfers between devices: 104 us -> none  [the longest x1 89.6 us: local(): first_whole = lax.all_gather(first_factor, 'dp', axis=1, tiled=True)]
    dot_general x11 -> x0, matrix products: 56.5 us -> none  [the longest x1 9.57 us: token_work(): back = jnp.dot(grads, output_weight.T, preferred_element_type=jnp.float32)]
    all_to_all x1 -> x0, waiting for transfers between devices: 15.1 us -> none  [local(): lax.all_to_all(d_mixed.reshape(local_rows, order, width), 'seq', split_ax...]
    convert_element_type x4 -> x0, local copies, waits for them, and re-layouts: 9.39 us -> none  [the longest x1 4.53 us: local(): mixed_cols = jnp.einsum('kla,akc->lkc', second_whole, first_cols, preferr...]
  transfers between devices with their start and end apart: 6 -> 0, of which waited for: 6 -> 0; matrix products, arithmetic and copies ran while one was open for 6% -> 0% of each run, Pallas kernels for 0% -> 0%
where the time goes in v2:
time: 363 us; the launch traced here: 359 us
  Pallas kernels  352 us (97%)
  local copies, waits for them, and re-layouts  6.91 us (2%)
    pallas_call x1, Pallas kernels, local(): pl.pallas_call(kernel, out_shape=(jax.ShapeDtypeStruct((1, 4096, 256), BF...  352 us

profile of v2, /device:TPU:89, one launch (start us, length us, event | category | flops | bytes accessed | tf_op | source)
XLA Modules:
  0.0 359.3 jit_solution(10250463725054314593)
XLA Ops:
  0.6 351.8 %shard_map.137 = (bf16[1,4096,256]{2,1,0:T(8,128)(2,1)}, bf16[8,128,512]{2,1,0:T(8,128)(2,1)}, bf16[8,128,512]{2,1,0:T(8,128)(2,1)}, f32[16,16,768]{2,1,0:T(8,128)}, f32[768,256]{1,0:T(8,128)}) custom-call(bf16[8,512,256]{2,1,0:T(8,128)(2,1)} %bitcast.4, bf16[8,512,256]{2,1,0:T(8,128)(2,1)} %bitcast.5, bf16[8,128,512]{2,1,0:T(8,128)(2,1)} %f_ref.1, ...), custom_call_target="tpu_custom_call" | custom-call | tf_op jit(solution)/shard_map/pallas_call | solution.py:526
  352.4 0.0 copy-start.1
  352.4 0.0 copy-start
  352.4 3.2 copy.20
  355.6 0.0 copy-done.1
  355.6 0.0 copy-start.3
  355.6 1.0 copy.21
  356.6 0.0 copy-done
  356.6 0.0 copy-start.2
  356.6 1.0 copy.22
  357.6 0.0 copy-done.3
  357.6 0.9 copy.23
  358.4 0.0 copy-done.2
  358.5 0.9 copy.24
Async XLA Ops:
  352.4 3.2 copy-start.1
  352.4 4.2 %copy-start = (bf16[8,128,512]{2,1,0:T(8,128)(2,1)S(1)}, bf16[8,128,512]{2,1,0:T(8,128)(2,1)}, u32[]{:S(2)}) copy-start(bf16[8,128,512]{2,1,0:T(8,128)(2,1)} %get-tuple-element.22) | copy-start | bytes 3145732
  355.6 1.9 copy-start.3
  356.6 1.9 copy-start.2

commit v3 on v2

--- a/solution.py
+++ b/solution.py
@@ -291,7 +291,7 @@
 
         loop(64, send)
 
-    for k in range(4):
+    for k in range(3):
         mate_mix(k)
     loop(8, own_tile, 4)
 
@@ -341,10 +341,11 @@
         drain(mb.at[1, :, k], four["a3_r"].at[k])
         d_columns(1, k)
 
-        def piece(t):
+        def piece(i):
+            t = (2 - base + i) % 4
             gb[k, t] = dot(dmk[k, rows_at(t * 128, 128), :], fmk[k], ((1,), (1,))).astype(BF)
 
-        loop(4, piece)
+        loop(2, piece)
         remote(gb.at[k, pl.ds(2 - base, 2)], gr.at[k], four["g_s"].at[k], four["g_r"].at[k], s, cross).start()
         first_back(1, k)
         pltpu.make_async_copy(dfb.at[1, s, k], dfr.at[1, s, k], four["a4_r"].at[k]).start()
@@ -354,6 +355,7 @@
             remote(dfb.at[1, t, k], dfr.at[1, s, k], four["a4_s"].at[k], four["a4_r"].at[k], t, p).start()
 
         loop(64, send, 1)
+        loop(4, piece, 2)
 
     def first_grad(k):
         drain(dfb.at[1, :, k], four["a4_r"].at[k])
@@ -367,8 +369,10 @@
         def block(a):
             fgb[k, :, a] = dot(dfa[a], xe[a], ((1,), (1,))).astype(BF).reshape(2, 32, 512)
 
-        loop(8, block)
-        remote(fgb.at[k, 1 - side], fgr.at[k], four["h_s"].at[k], four["h_r"].at[k], s, cross).start()
+        for part in (0, 4):
+            loop(part + 4, block, part)
+            away = fgb.at[k, 1 - side, pl.ds(part, 4)]
+            remote(away, fgr.at[k, pl.ds(part, 4)], four["h_s"].at[k], four["h_r"].at[k], s, cross).start()
 
     def second_sum(k):
         drain(gr.at[k], four["g_r"].at[k])
@@ -418,6 +422,7 @@
 
     own_back()
     mate_tokens(0)
+    mate_mix(3)
     mate_tokens(1)
     mate_back(0)
     mate_tokens(2)

time: 363 us -> 360 us (level); the launches traced: 359 us -> 360 us
  no operation moved by 1% of the time
where the time goes in v3:
time: 360 us
  Pallas kernels  352 us (98%)
  local copies, waits for them, and re-layouts  6.91 us (2%)
    pallas_call x1, Pallas kernels, local(): pl.pallas_call(kernel, out_shape=(jax.ShapeDtypeStruct((1, 4096, 256), BF...  352 us

profile of v3, /device:TPU:89, one launch (start us, length us, event | category | flops | bytes accessed | tf_op | source)
XLA Modules:
  0.0 360.0 jit_solution(1825572879872123586)
XLA Ops:
  0.6 352.5 %shard_map.137 = (bf16[1,4096,256]{2,1,0:T(8,128)(2,1)}, bf16[8,128,512]{2,1,0:T(8,128)(2,1)}, bf16[8,128,512]{2,1,0:T(8,128)(2,1)}, f32[16,16,768]{2,1,0:T(8,128)}, f32[768,256]{1,0:T(8,128)}) custom-call(bf16[8,512,256]{2,1,0:T(8,128)(2,1)} %bitcast.4, bf16[8,512,256]{2,1,0:T(8,128)(2,1)} %bitcast.5, bf16[8,128,512]{2,1,0:T(8,128)(2,1)} %f_ref.1, ...), custom_call_target="tpu_custom_call" | custom-call | tf_op jit(solution)/shard_map/pallas_call | solution.py:531
  353.1 0.0 copy-start.1
  353.1 0.0 copy-start
  353.1 3.2 copy.20
  356.3 0.0 copy-done.1
  356.3 0.0 copy-start.3
  356.3 1.0 copy.21
  357.3 0.0 copy-done
  357.3 0.0 copy-start.2
  357.3 1.0 copy.22
  358.3 0.0 copy-done.3
  358.3 0.9 copy.23
  359.1 0.0 copy-done.2
  359.1 0.9 copy.24
Async XLA Ops:
  353.1 3.2 copy-start.1
  353.1 4.2 %copy-start = (bf16[8,128,512]{2,1,0:T(8,128)(2,1)S(1)}, bf16[8,128,512]{2,1,0:T(8,128)(2,1)}, u32[]{:S(2)}) copy-start(bf16[8,128,512]{2,1,0:T(8,128)(2,1)} %get-tuple-element.22) | copy-start | bytes 3145732
  356.3 1.9 copy-start.3
  357.3 1.9 copy-start.2

commit v4 on v3

--- a/solution.py
+++ b/solution.py
@@ -199,10 +199,10 @@
 
     load_f.wait()
     drain(f2.at[:, 1 - side], one["f_r"])
-    first_mix(0, 0, 256)
     drain(sp.at[:, pl.ds(0, 2)], one["sa_r"])
     half = sp.at[:, pl.ds(base, 2)]
     remote(half, half, one["sb_s"], one["sb_r"], s, cross).start()
+    first_mix(0, 0, 256)
     x_half(0).wait_send()
     x_half(1).start()
     x_half(0).wait_recv()

time: 360 us -> 358 us (level)
  Pallas kernels: 352 us -> 347 us
    pallas_call x1, Pallas kernels: 352 us -> 347 us  [local(): pl.pallas_call(kernel, out_shape=(jax.ShapeDtypeStruct((1, 4096, 256), BF...]
where the time goes in v4:
time: 358 us; the launch traced here: 355 us
  Pallas kernels  347 us (97%)
  local copies, waits for them, and re-layouts  6.91 us (2%)
    pallas_call x1, Pallas kernels, local(): pl.pallas_call(kernel, out_shape=(jax.ShapeDtypeStruct((1, 4096, 256), BF...  347 us

profile of v4, /device:TPU:89, one launch (start us, length us, event | category | flops | bytes accessed | tf_op | source)
XLA Modules:
  0.0 354.9 jit_solution(6504249355167410887)
XLA Ops:
  0.6 347.4 %shard_map.137 = (bf16[1,4096,256]{2,1,0:T(8,128)(2,1)}, bf16[8,128,512]{2,1,0:T(8,128)(2,1)}, bf16[8,128,512]{2,1,0:T(8,128)(2,1)}, f32[16,16,768]{2,1,0:T(8,128)}, f32[768,256]{1,0:T(8,128)}) custom-call(bf16[8,512,256]{2,1,0:T(8,128)(2,1)} %bitcast.4, bf16[8,512,256]{2,1,0:T(8,128)(2,1)} %bitcast.5, bf16[8,128,512]{2,1,0:T(8,128)(2,1)} %f_ref.1, ...), custom_call_target="tpu_custom_call" | custom-call | tf_op jit(solution)/shard_map/pallas_call | solution.py:531
  348.0 0.0 copy-start.1
  348.0 0.0 copy-start
  348.0 3.2 copy.20
  351.2 0.0 copy-done.1
  351.2 0.0 copy-start.3
  351.2 1.0 copy.21
  352.2 0.0 copy-done
  352.2 0.0 copy-start.2
  352.2 1.0 copy.22
  353.2 0.0 copy-done.3
  353.2 0.9 copy.23
  354.1 0.0 copy-done.2
  354.1 0.9 copy.24
Async XLA Ops:
  348.0 3.2 copy-start.1
  348.0 4.2 %copy-start = (bf16[8,128,512]{2,1,0:T(8,128)(2,1)S(1)}, bf16[8,128,512]{2,1,0:T(8,128)(2,1)}, u32[]{:S(2)}) copy-start(bf16[8,128,512]{2,1,0:T(8,128)(2,1)} %get-tuple-element.22) | copy-start | bytes 3145732
  351.2 1.9 copy-start.3
  352.2 1.9 copy-start.2
